TPU v7x, 32 devices: a whole 2x2x4 slice. The times are simulated.
32 devices in a mesh: groups: 2 (over x), wide: 16 (over z, y, core).
Axes of the slice: x: 2, y: 2, z: 4, core: 2. Of those that a mesh axis runs over, the one named last changes fastest.
Arguments:
- hidden: bfloat16 [256, 28672], P('groups', 'wide'), parts along dimension 0, may hold values from -6 to 6
- adapter_ids: int32 [256], P('groups'), parts along dimension 0, may hold values from 0 to 31, as said below
- core_slot: int32 [64], P('groups'), parts along dimension 0, may hold values from 0 to 31, as said below
- down_weight: bfloat16 [16, 3584, 6144], P('wide'), may hold values from -0.03125 to 0.03125
- rank_in: bfloat16 [28672, 512], P('wide'), may hold values from -0.03125 to 0.03125
- rank_out: bfloat16 [16, 64, 6144], P('wide'), may hold values from -0.25 to 0.25
- cores: bfloat16 [32, 512, 512], P('wide'), may hold values from -0.25 to 0.25
Outputs:
- layer_out: bfloat16 [256, 12288], P(('groups', 'wide')), parts along dimension 0
There are 2 independent parts, one for each index of `groups`. A program takes and returns all parts, laid end to end along the dimension named above; an argument that names none is the same for every part. Nothing has to cross between parts.
Inputs may be any that keep to these rules, and one draw needn't show every extreme that they name: core_slot is a permutation of the 32 adapters. `adapter_ids`: at most 32 tokens use adapters whose core rows lie in one block of 2 rows of cores (rows j * 2 to j * 2 + 1), and some block takes exactly 32.
All inputs are finite; a program needn't handle non-finite values.
Results may differ from a plain program's by a relative error of at most 0.005.
Values may be sent and summed in bfloat16 or wider, within the bound.
A program may use at most 128 MiB of HBM per device.

v0:
```python
import jax
import jax.numpy as jnp
from jax import lax
from jax.sharding import PartitionSpec as P

FF_GROUPS = 8


def swapped(value, axis, distance):
    return lax.ppermute(value, axis, [(i, i ^ 1 << distance) for i in range(lax.axis_size(axis))])


def bit_value(device, bit_index):
    return device // (1 << bit_index) % 2


def shards(hidden, adapter_ids, core_slot, down_weight, rank_in, rank_out, cores):
    devices = lax.axis_size("wide")
    device = lax.axis_index("wide")
    token_count = hidden.shape[0]
    rows_own = token_count // devices
    rank_size = rank_in.shape[1]
    slice_width = rank_size // devices
    adapters_all = core_slot.shape[0]
    column_groups = devices // FF_GROUPS
    low_bits = column_groups.bit_length() - 1
    block_width = down_weight.shape[2]
    partial_rank = jnp.dot(hidden, rank_in, preferred_element_type=jnp.float32)
    projected = lax.psum(partial_rank, "wide").astype(jnp.bfloat16)
    hidden_pieces = hidden
    for bit_index in range(low_bits):
        partner = swapped(hidden_pieces, "wide", bit_index)
        high_side = bit_value(device, bit_index) == 1
        hidden_pieces = jnp.where(
            high_side,
            jnp.concatenate([partner, hidden_pieces], 1),
            jnp.concatenate([hidden_pieces, partner], 1),
        )
    matches = adapter_ids[:, None] == jnp.arange(adapters_all, dtype=jnp.int32)[None, :]
    token_slot = jnp.sum(jnp.where(matches, core_slot[None, :], 0), axis=1)
    turned = jnp.transpose(cores, (1, 0, 2))
    columns = lax.all_to_all(turned, "wide", split_axis=2, concat_axis=1, tiled=True)
    products = jnp.dot(
        projected,
        columns.reshape(rank_size, adapters_all * slice_width),
        preferred_element_type=jnp.float32,
    )
    products = products.reshape(token_count, adapters_all, slice_width)
    picked = token_slot[:, None] == jnp.arange(adapters_all, dtype=jnp.int32)[None, :]
    lowrank = jnp.sum(jnp.where(picked[:, :, None], products, jnp.float32(0.0)), axis=1).astype(
        jnp.bfloat16
    )
    rank_pieces = lowrank
    for bit_index in range(low_bits):
        partner = swapped(rank_pieces, "wide", bit_index)
        high_side = bit_value(device, bit_index) == 1
        rank_pieces = jnp.where(
            high_side,
            jnp.concatenate([partner, rank_pieces], 1),
            jnp.concatenate([rank_pieces, partner], 1),
        )
    partial_value = jnp.dot(hidden_pieces, down_weight[0], preferred_element_type=jnp.float32)
    partial_value = partial_value + jnp.dot(
        rank_pieces, rank_out[0], preferred_element_type=jnp.float32
    )
    outgoing = partial_value.reshape(devices, rows_own, block_width)
    received = lax.all_to_all(outgoing, "wide", split_axis=0, concat_axis=0, tiled=True)
    summed = jnp.sum(received.reshape(FF_GROUPS, column_groups, rows_own, block_width), axis=0)
    layer_out = jnp.transpose(summed, (1, 0, 2)).reshape(rows_own, column_groups * block_width)
    return layer_out.astype(jnp.bfloat16)


def solution(mesh):
    return jax.shard_map(
        shards,
        mesh=mesh,
        in_specs=(
            P("groups", "wide"),
            P("groups"),
            P("groups"),
            P("wide", None, None),
            P("wide", None),
            P("wide", None, None),
            P("wide", None, None),
        ),
        out_specs=P(("groups", "wide"), None),
        check_vma=False,
    )
```

profile of v0, /device:TPU:1, one launch (start us, length us, event | category | flops | bytes accessed | tf_op | source)
XLA Modules:
  0.0 190.2 jit_solution(9479512025097720160)
XLA Ops:
  0.0 0.0 copy-start
  0.0 0.0 copy-start.1
  0.0 0.0 copy-start.3
  0.0 0.0 copy-start.4
  0.0 3.8 %copy.15 = bf16[2,512,512]{1,0,2:T(2,128)(2,1)} copy(bf16[2,512,512]{2,1,0:T(8,128)(2,1)} %param.13) | data formatting | bytes 2097152 | tf_op args[6]
  3.8 7.3 %all-to-all-start = ((bf16[512,2,512]{0,1,2:T(2,128)(2,1)}), bf16[512,2,512]{0,1,2:T(2,128)(2,1)S(1)}, u32[]{:S(2)}, u32[]{:S(2)}) async-start(bf16[512,2,512]{0,1,2:T(2,128)(2,1)} %bitcast.32), calls=%async_computation | async-start | bytes 2097152 | tf_op jit(solution)/shard_map/all_to_all | solution.py:42
  11.2 0.0 copy-done.1
  11.2 0.2 collective-permute-start
  11.4 0.0 copy-done
  11.4 1.1 fusion.27
  12.5 0.0 copy-done.3
  12.5 0.0 copy-done.4
  12.5 0.1 select_reduce_fusion
  12.6 69.0 %all-reduce.1 = bf16[128,512]{1,0:T(8,128)(2,1)S(1)} all-reduce(f32[128,512]{1,0:T(8,128)} %fusion.27), channel_id=1, replica_groups=mesh['groups'=2,'wide'=16] {'wide'}, use_global_device_ids=true, to_apply=%region_1.2 | all-reduce | flops 65536 | bytes 393216 | tf_op jit(solution)/shard_map/psum | solution.py:29
  81.6 0.0 all-to-all-done
  81.7 0.2 copy.16
  81.8 0.0 copy-start.2
  81.8 0.1 copy.17
  82.0 0.4 fusion.8
  82.4 5.1 %collective-permute-start.1 = (bf16[128,32]{0,1:T(8,128)(2,1)S(1)}, bf16[128,32]{0,1:T(8,128)(2,1)S(1)}, u32[]{:S(2)}, u32[]{:S(2)}) collective-permute-start(bf16[128,32]{0,1:T(8,128)(2,1)S(1)} %fusion.8), channel_id=1, source_target_pairs={{0,1},{1,0},{2,3},{3,2},{4,5},{5,4},{6,7},{7,6},{8,9},{9,8},{10,11... | collective-permute-start | bytes 24584 | tf_op jit(solution)/shard_map/ppermute | solution.py:10
  87.5 0.8 collective-permute-done.1
  88.4 0.0 copy-done.2
  88.4 2.3 %fusion.15 = f32[128,6144]{1,0:T(8,128)} fusion(bf16[1,64,6144]{2,1,0:T(8,128)(2,1)S(1)} %copy-done.2, bf16[128,32]{0,1:T(8,128)(2,1)S(1)} %fusion.8, bf16[128,32]{0,1:T(8,128)(2,1)S(1)} %collective-permute-done.1, pred[]{:T(512)S(6)} %eq.37), kind=kOutput, calls=%fused_computation.13 | convolution fusion | flops 100737024 | bytes 3948545 | tf_op jit(solution)/shard_map/dot_general | solution.py:63
  90.7 0.0 collective-permute-done
  90.7 21.9 %fusion.5 = f32[16,8,6144]{2,1,0:T(8,128)} fusion(f32[128,6144]{1,0:T(8,128)} %fusion.15, bf16[1,3584,6144]{2,1,0:T(8,128)(2,1)} %param.10, bf16[128,1792]{1,0:T(8,128)(2,1)S(1)} %copy-done.1, bf16[128,1792]{1,0:T(8,128)(2,1)} %collective-permute-done, pred[]{:T(512)S(6)} %eq.37), kind=kOutput, calls=%fused_computation.3 | convolution fusion | flops 5642059776 | bytes 51249152 | tf_op jit(solution)/shard_map/dot_general | solution.py:62
  112.6 74.8 %all_to_all.20 = f32[16,8,6144]{2,1,0:T(8,128)} all-to-all(f32[16,8,6144]{2,1,0:T(8,128)} %fusion.5), channel_id=1, replica_groups=mesh['groups'=2,'wide'=16] {'wide'}, dimensions={0} | all-to-all | bytes 6291456 | tf_op jit(solution)/shard_map/all_to_all | solution.py:67
  187.5 2.8 %reduce_sum.29 = bf16[2,8,6144]{2,1,0:T(8,128)(2,1)} reduce(f32[8,2,8,6144]{3,2,1,0:T(8,128)} %bitcast.31, f32[]{:T(128)} %constant.34.clone.1), dimensions={0}, to_apply=%region_3.4 | reduce | flops 688128 | bytes 3342340 | tf_op jit(solution)/shard_map/reduce_sum | solution.py:68
  (1 shorter events, 0.0 us)
Async XLA Ops:
  0.0 11.4 %copy-start = (bf16[1792,512]{1,0:T(8,128)(2,1)S(1)}, bf16[1792,512]{1,0:T(8,128)(2,1)}, u32[]{:S(2)}) copy-start(bf16[1792,512]{1,0:T(8,128)(2,1)} %param.11) | copy-start | bytes 5505028
  0.0 11.2 %copy-start.1 = (bf16[128,1792]{1,0:T(8,128)(2,1)S(1)}, bf16[128,1792]{1,0:T(8,128)(2,1)}, u32[]{:S(2)}) copy-start(bf16[128,1792]{1,0:T(8,128)(2,1)} %param.7) | copy-start | bytes 1376260
  0.0 12.5 %copy-start.3 = (s32[32]{0:T(128)S(1)}, s32[32]{0:T(128)}, u32[]{:S(2)}) copy-start(s32[32]{0:T(128)} %param.9) | copy-start | bytes 388
  0.0 12.5 %copy-start.4 = (s32[128]{0:T(128)S(1)}, s32[128]{0:T(128)}, u32[]{:S(2)}) copy-start(s32[128]{0:T(128)} %param.8) | copy-start | bytes 1540
  3.8 77.8 %all-to-all-start = ((bf16[512,2,512]{0,1,2:T(2,128)(2,1)}), bf16[512,2,512]{0,1,2:T(2,128)(2,1)S(1)}, u32[]{:S(2)}, u32[]{:S(2)}) async-start(bf16[512,2,512]{0,1,2:T(2,128)(2,1)} %bitcast.32), calls=%async_computation | async-start | bytes 2097152 | tf_op jit(solution)/shard_map/all_to_all | solution.py:42
  11.2 79.5 %collective-permute-start = (bf16[128,1792]{1,0:T(8,128)(2,1)S(1)}, bf16[128,1792]{1,0:T(8,128)(2,1)}, u32[]{:S(2)}, u32[]{:S(2)}) collective-permute-start(bf16[128,1792]{1,0:T(8,128)(2,1)S(1)} %copy-done.1), channel_id=1, source_target_pairs={{0,1},{1,0},{2,3},{3,2},{4,5},{5,4},{6,7},{7,6},{8,9},{9,8},{10,11... | collective-permute-start | bytes 1376264 | tf_op jit(solution)/shard_map/ppermute | solution.py:10
  81.8 6.5 %copy-start.2 = (bf16[1,64,6144]{2,1,0:T(8,128)(2,1)S(1)}, bf16[1,64,6144]{2,1,0:T(8,128)(2,1)}, u32[]{:S(2)}) copy-start(bf16[1,64,6144]{2,1,0:T(8,128)(2,1)} %param.12) | copy-start | bytes 2359300
  82.4 6.0 %collective-permute-start.1 = (bf16[128,32]{0,1:T(8,128)(2,1)S(1)}, bf16[128,32]{0,1:T(8,128)(2,1)S(1)}, u32[]{:S(2)}, u32[]{:S(2)}) collective-permute-start(bf16[128,32]{0,1:T(8,128)(2,1)S(1)} %fusion.8), channel_id=1, source_target_pairs={{0,1},{1,0},{2,3},{3,2},{4,5},{5,4},{6,7},{7,6},{8,9},{9,8},{10,11... | collective-permute-start | bytes 24584 | tf_op jit(solution)/shard_map/ppermute | solution.py:10
where the time goes:
time: 191 us; the launch traced here: 190 us
  blocking collectives  144 us (75%)
  matrix products  25.8 us (14%)
  starting transfers between devices  12.7 us (7%)
  local copies, waits for them, and re-layouts  4.1 us (2%)
  other arithmetic  2.87 us (2%)
    all_to_all x1, blocking collectives, shards(): lax.all_to_all(outgoing, 'wide', split_axis=0, concat_axis=0, tiled=True)  74.8 us
    psum x1, blocking collectives, shards(): projected = lax.psum(partial_rank, 'wide').astype(jnp.bfloat16)  69 us
    dot_general x1, matrix products, shards(): jnp.dot(hidden_pieces, down_weight[0], preferred_element_type=jnp.float32)  21.9 us
    all_to_all x1, starting transfers between devices, shards(): lax.all_to_all(turned, 'wide', split_axis=2, concat_axis=1, tiled=True)  7.35 us
    ppermute x2, starting transfers between devices, swapped(): lax.ppermute(value, axis, [(i, i ^ 1 << distance) for i in range(lax.axis...  5.31 us
    unnamed x11, local copies, waits for them, and re-layouts  3.83 us
  transfers between devices with their start and end apart: 3, of which 1 were waited for; matrix products, arithmetic and copies ran while one was open for 2% of the time, Pallas kernels for 0%

commit v1 on v0

--- a/solution.py
+++ b/solution.py
@@ -1,9 +1,12 @@
 import jax
 import jax.numpy as jnp
 from jax import lax
+from jax.experimental import pallas as pl
+from jax.experimental.pallas import tpu as pltpu
 from jax.sharding import PartitionSpec as P
 
 FF_GROUPS = 8
+WINDOW = 3
 
 
 def swapped(value, axis, distance):
@@ -14,7 +17,7 @@
     return device // (1 << bit_index) % 2
 
 
-def shards(hidden, adapter_ids, core_slot, down_weight, rank_in, rank_out, cores):
+def general(hidden, adapter_ids, core_slot, down_weight, rank_in, rank_out, cores):
     devices = lax.axis_size("wide")
     device = lax.axis_index("wide")
     token_count = hidden.shape[0]
@@ -63,11 +66,356 @@
     partial_value = partial_value + jnp.dot(
         rank_pieces, rank_out[0], preferred_element_type=jnp.float32
     )
-    outgoing = partial_value.reshape(devices, rows_own, block_width)
+    outgoing = partial_value.astype(jnp.bfloat16).reshape(devices, rows_own, block_width)
     received = lax.all_to_all(outgoing, "wide", split_axis=0, concat_axis=0, tiled=True)
-    summed = jnp.sum(received.reshape(FF_GROUPS, column_groups, rows_own, block_width), axis=0)
+    received = received.reshape(FF_GROUPS, column_groups, rows_own, block_width)
+    summed = jnp.sum(received.astype(jnp.float32), axis=0)
     layer_out = jnp.transpose(summed, (1, 0, 2)).reshape(rows_own, column_groups * block_width)
     return layer_out.astype(jnp.bfloat16)
+
+
+CHUNK = 768
+HELD = 6
+OWNER_CAP = 32
+MESH = pl.DeviceIdType.MESH
+F32, BF16 = jnp.float32, jnp.bfloat16
+
+
+def remote(src, dst, send, recv, target):
+    return pltpu.make_async_remote_copy(
+        src_ref=src, dst_ref=dst, send_sem=send, recv_sem=recv, device_id={"wide": target}, device_id_type=MESH
+    )
+
+
+def kernel(
+    ids_col, ids_row, slot_col, slot_row, hidden, weight, rank_in, rank_out, cores, out,
+    hid, wbuf, rin, core_buf, vbuf, acc, pstage, precv, proj, projected, lstage, lrecv,
+    ystage, yrecv, zstage, zrecv, fin, frecv,
+    load_sem, w_sem, h_sem, ps_sem, pr_sem, as_sem, ar_sem, ls_sem, lr_sem,
+    ys_sem, yr_sem, zs_sem, zr_sem, fs_sem, fr_sem,
+):
+    n = 2 * FF_GROUPS
+    me = lax.axis_index("wide")
+    side = lax.rem(me, 2)
+    group = lax.div(me, 2)
+    yy = lax.rem(group, 2)
+    zz = lax.div(group, 2)
+    sibling = me + 1 - 2 * side
+    y_partner = me + 2 - 4 * yy
+    chunks = wbuf.shape[0]
+    tokens = hid.shape[0]
+    units = hidden.shape[1]
+    rank_rows = rank_out.shape[1]
+    own_units = pl.ds(pl.multiple_of(side * units, 128), units)
+    adapters = cores.shape[0]
+
+    def w_copy(k):
+        cols = pl.ds(pl.multiple_of(k * CHUNK, CHUNK), CHUNK)
+        return pltpu.make_async_copy(weight.at[0, :, cols], wbuf.at[k], w_sem.at[k])
+
+    hid_copy = pltpu.make_async_copy(hidden, hid.at[:, own_units], load_sem.at[0])
+    hid_copy.start()
+    rin_copy = pltpu.make_async_copy(rank_in, rin, load_sem.at[1])
+    rin_copy.start()
+    for k in range(WINDOW):
+        w_copy(k).start()
+    core_copy = pltpu.make_async_copy(cores, core_buf, load_sem.at[2])
+    core_copy.start()
+    half = lax.rem(group, 2)
+    spare = pl.ds(pl.multiple_of((1 - half) * rank_rows, rank_rows), rank_rows)
+    vbuf[spare, :] = jnp.zeros((rank_rows, vbuf.shape[1]), BF16)
+    own_rank = pl.ds(pl.multiple_of(half * rank_rows, rank_rows), rank_rows)
+    v_copy = pltpu.make_async_copy(rank_out.at[0], vbuf.at[own_rank, :], load_sem.at[3])
+    v_copy.start()
+
+    barrier = pltpu.get_barrier_semaphore()
+
+    @pl.loop(1, n)
+    def _(d):
+        pl.semaphore_signal(barrier, inc=1, device_id={"wide": lax.rem(me + d, n)}, device_id_type=MESH)
+
+    pl.semaphore_wait(barrier, n - 1)
+
+    hid_copy.wait()
+    h_send = remote(hid.at[:, own_units], hid.at[:, own_units], h_sem.at[0], h_sem.at[1], sibling)
+    h_send.start()
+
+    rin_copy.wait()
+    partial_rank = jnp.dot(hid[:, own_units], rin[...], preferred_element_type=F32).astype(BF16)
+    for c in range(FF_GROUPS):
+        for s in range(2):
+            pstage[2 * c + s] = partial_rank[16 * c : 16 * c + 16, 256 * s : 256 * s + 256]
+
+    def p_copy(d):
+        target = lax.rem(me + d, n)
+        return remote(pstage.at[target], precv.at[me], ps_sem.at[target], pr_sem.at[me], target)
+
+    def p_arrival(d):
+        source = lax.rem(me + d, n)
+        return remote(pstage.at[me], precv.at[source], ps_sem.at[source], pr_sem.at[source], source)
+
+    @pl.loop(1, n)
+    def _(d):
+        p_copy(d).start()
+
+    precv[me] = pstage[me]
+
+    def start_next(k):
+        @pl.when(k + WINDOW < chunks)
+        def _():
+            w_copy(k + WINDOW).start()
+
+    def product(k):
+        w_copy(k).wait()
+        start_next(k)
+        return jnp.dot(hid[...], wbuf[k], preferred_element_type=F32)
+
+    def hold(first, last):
+        @pl.loop(first, last)
+        def _(k):
+            acc[k] = product(k)
+
+    def number(mask):
+        return jnp.where(mask, 1.0, 0.0)
+
+    all_a = slot_col.shape[0]
+    lanes_a = lax.broadcasted_iota(jnp.int32, (tokens, all_a), 1)
+    rows_a = lax.broadcasted_iota(jnp.int32, (all_a, tokens), 0)
+    slots_c = jnp.sum(
+        jnp.where(ids_col[...] == lanes_a, slot_row[...].astype(F32), 0.0), axis=1, keepdims=True
+    ).astype(jnp.int32)
+    slots_r = jnp.sum(
+        jnp.where(ids_row[...] == rows_a, slot_col[...].astype(F32), 0.0), axis=0, keepdims=True
+    ).astype(jnp.int32)
+    owner_c = lax.div(slots_c, jnp.int32(adapters))
+    owner_r = lax.div(slots_r, jnp.int32(adapters))
+    sub = lax.broadcasted_iota(jnp.int32, (tokens, tokens), 0)
+    lane = lax.broadcasted_iota(jnp.int32, (tokens, tokens), 1)
+    same = owner_c == owner_r
+    place_c = jnp.sum(number(same & (lane < sub)), axis=1, keepdims=True).astype(jnp.int32)
+    place_r = jnp.sum(number(same & (sub < lane)), axis=0, keepdims=True).astype(jnp.int32)
+    rows_p = lax.broadcasted_iota(jnp.int32, (OWNER_CAP, tokens), 0)
+    mine = number((owner_r == me) & (place_r == rows_p))
+    picked_slot = jnp.sum(mine * slots_r.astype(F32), axis=1, keepdims=True).astype(jnp.int32)
+    lanes_s = lax.broadcasted_iota(jnp.int32, (tokens, n * OWNER_CAP), 1)
+
+    h_send.wait()
+    hold(0, 2)
+
+    @pl.loop(1, n)
+    def _(d):
+        p_arrival(d).wait_recv()
+
+    total = precv[0].astype(F32)
+    for s in range(1, n):
+        total += precv[s].astype(F32)
+    proj[me] = total.astype(BF16)
+
+    def a_copy(d):
+        target = lax.rem(me + d, n)
+        return remote(proj.at[me], proj.at[me], as_sem.at[target], ar_sem.at[me], target)
+
+    def a_arrival(d):
+        source = lax.rem(me + d, n)
+        return remote(proj.at[source], proj.at[source], as_sem.at[source], ar_sem.at[source], source)
+
+    @pl.loop(1, n)
+    def _(d):
+        a_copy(d).start()
+
+    hold(2, 4)
+
+    @pl.loop(1, n)
+    def _(d):
+        a_arrival(d).wait_recv()
+
+    for c in range(FF_GROUPS):
+        for s in range(2):
+            projected[16 * c : 16 * c + 16, 256 * s : 256 * s + 256] = proj[2 * c + s]
+    core_copy.wait()
+    own = jnp.dot(mine.astype(BF16), projected[...], preferred_element_type=F32).astype(BF16)
+    low = jnp.zeros(own.shape, F32)
+    for a in range(adapters):
+        term = jnp.dot(own, core_buf[a], preferred_element_type=F32)
+        low = jnp.where(picked_slot == me * adapters + a, term, low)
+    low = low.astype(BF16)
+    for s in range(lstage.shape[0]):
+        lstage[s] = low[:, 128 * s : 128 * s + 128]
+
+    def l_copy(d):
+        target = lax.rem(me + d, n)
+        return remote(lstage.at[lax.div(target, 4)], lrecv.at[me], ls_sem.at[target], lr_sem.at[me], target)
+
+    def l_arrival(d):
+        source = lax.rem(me + d, n)
+        return remote(lstage.at[0], lrecv.at[source], ls_sem.at[source], lr_sem.at[source], source)
+
+    @pl.loop(1, n)
+    def _(d):
+        l_copy(d).start()
+
+    lrecv[me] = lstage[lax.div(me, 4)]
+    hold(4, HELD)
+
+    @pl.loop(1, n)
+    def _(d):
+        l_arrival(d).wait_recv()
+
+    expand = number(owner_c * OWNER_CAP + place_c == lanes_s).astype(BF16)
+    arrived = lrecv[...].reshape(n * OWNER_CAP, 128)
+    lowrank = jnp.dot(expand, arrived, preferred_element_type=F32).astype(BF16)
+    v_copy.wait()
+
+    def y_copy(k):
+        return remote(ystage.at[k, 1 - yy], yrecv.at[k], ys_sem.at[k], yr_sem.at[k], y_partner)
+
+    def send_y(k, value):
+        cols = pl.ds(pl.multiple_of(k * CHUNK, CHUNK), CHUNK)
+        value = (value + jnp.dot(lowrank, vbuf[:, cols], preferred_element_type=F32)).astype(BF16)
+        for c in range(FF_GROUPS):
+            ystage[k, c % 2, c // 2] = value[16 * c : 16 * c + 16]
+        y_copy(k).start()
+
+    def z_copy(k, d):
+        z_to = lax.rem(zz + d, 4)
+        return remote(
+            zstage.at[k, z_to], zrecv.at[k, zz], zs_sem.at[k, z_to], zr_sem.at[k, zz], z_to * 4 + lax.rem(me, 4)
+        )
+
+    def z_arrival(k, d):
+        z_from = lax.rem(zz + d, 4)
+        return remote(
+            zstage.at[k, zz], zrecv.at[k, z_from], zs_sem.at[k, z_from], zr_sem.at[k, z_from], z_from * 4 + lax.rem(me, 4)
+        )
+
+    def turn(k):
+        y_copy(k).wait_recv()
+        zstage[k] = (ystage[k, yy].astype(F32) + yrecv[k].astype(F32)).astype(BF16)
+        for d in range(1, 4):
+            z_copy(k, d).start()
+        zrecv[k, zz] = zstage[k, zz]
+
+    def f_copy(k):
+        return remote(fin.at[k], frecv.at[k], fs_sem.at[k], fr_sem.at[k], sibling)
+
+    def finish(k):
+        for d in range(1, 4):
+            z_arrival(k, d).wait_recv()
+        fin[k] = jnp.sum(zrecv[k].astype(F32), axis=0).astype(BF16)
+        f_copy(k).start()
+
+    @pl.loop(0, HELD)
+    def _(k):
+        send_y(k, acc[k])
+
+    @pl.loop(HELD, chunks)
+    def _(k):
+        send_y(k, product(k))
+        turn(k - HELD)
+
+    turned = chunks - HELD
+
+    @pl.loop(turned, chunks)
+    def _(k):
+        turn(k)
+        finish(k - turned)
+
+    @pl.loop(chunks - turned, chunks)
+    def _(k):
+        finish(k)
+
+    def rows_of(value):
+        value = value.astype(F32)
+        rows = value.shape[0] // 2
+        return jnp.where(side == 0, value[:rows], value[rows:]).astype(out.dtype)
+
+    @pl.loop(0, chunks)
+    def _(k):
+        f_copy(k).wait_recv()
+        left = pl.multiple_of(side * (chunks * CHUNK) + k * CHUNK, 128)
+        right = pl.multiple_of((1 - side) * (chunks * CHUNK) + k * CHUNK, 128)
+        out[:, pl.ds(left, CHUNK)] = rows_of(fin[k])
+        out[:, pl.ds(right, CHUNK)] = rows_of(frecv[k])
+
+    @pl.loop(1, n)
+    def _(d):
+        p_copy(d).wait_send()
+        a_copy(d).wait_send()
+        l_copy(d).wait_send()
+
+    @pl.loop(0, chunks)
+    def _(k):
+        y_copy(k).wait_send()
+        f_copy(k).wait_send()
+        for d in range(1, 4):
+            z_copy(k, d).wait_send()
+
+
+def fused(hidden, adapter_ids, core_slot, down_weight, rank_in, rank_out, cores):
+    n = lax.axis_size("wide")
+    tokens, units = hidden.shape
+    rows, width = down_weight.shape[1:]
+    chunks = width // CHUNK
+    rank = rank_in.shape[1]
+    adapters = core_slot.shape[0]
+    anywhere = pl.BlockSpec(memory_space=pl.ANY)
+    local = pl.BlockSpec(memory_space=pltpu.VMEM)
+    dma = pltpu.SemaphoreType.DMA
+    return pl.pallas_call(
+        kernel,
+        out_shape=jax.ShapeDtypeStruct((tokens // n, 2 * width), BF16),
+        in_specs=[local] * 4 + [anywhere] * 5,
+        out_specs=local,
+        scratch_shapes=[
+            pltpu.VMEM((tokens, rows), BF16),
+            pltpu.VMEM((chunks, rows, CHUNK), BF16),
+            pltpu.VMEM(rank_in.shape, BF16),
+            pltpu.VMEM(cores.shape, BF16),
+            pltpu.VMEM((128, width), BF16),
+            pltpu.VMEM((HELD, tokens, CHUNK), F32),
+            pltpu.VMEM((n, 16, rank // 2), BF16),
+            pltpu.VMEM((n, 16, rank // 2), BF16),
+            pltpu.VMEM((n, 16, rank // 2), BF16),
+            pltpu.VMEM((tokens, rank), BF16),
+            pltpu.VMEM((rank // 128, OWNER_CAP, 128), BF16),
+            pltpu.VMEM((n, OWNER_CAP, 128), BF16),
+            pltpu.VMEM((chunks, 2, 4, 16, CHUNK), BF16),
+            pltpu.VMEM((chunks, 4, 16, CHUNK), BF16),
+            pltpu.VMEM((chunks, 4, 16, CHUNK), BF16),
+            pltpu.VMEM((chunks, 4, 16, CHUNK), BF16),
+            pltpu.VMEM((chunks, 16, CHUNK), BF16),
+            pltpu.VMEM((chunks, 16, CHUNK), BF16),
+            dma((4,)), dma((chunks,)), dma((2,)),
+            dma((n,)), dma((n,)), dma((n,)), dma((n,)), dma((n,)), dma((n,)),
+            dma((chunks,)), dma((chunks,)), dma((chunks, 4)), dma((chunks, 4)),
+            dma((chunks,)), dma((chunks,)),
+        ],
+        compiler_params=pltpu.CompilerParams(
+            collective_id=0, has_side_effects=True, vmem_limit_bytes=60 * 1024 * 1024
+        ),
+        cost_estimate=pl.CostEstimate(
+            flops=2 * tokens * rows * width, bytes_accessed=2 * rows * width, transcendentals=0
+        ),
+    )(
+        adapter_ids.reshape(tokens, 1), adapter_ids.reshape(1, tokens),
+        core_slot.reshape(adapters, 1), core_slot.reshape(1, adapters),
+        hidden, down_weight, rank_in, rank_out, cores,
+    )
+
+
+def fits(devices, args):
+    hidden, down_weight, rank_in = args[0], args[3], args[4]
+    return (
+        devices == 2 * FF_GROUPS
+        and hidden.shape[0] == 16 * FF_GROUPS
+        and rank_in.shape[1] == 64 * FF_GROUPS
+        and down_weight.shape[2] % CHUNK == 0
+        and down_weight.shape[2] // CHUNK >= HELD
+    )
+
+
+def shards(*args):
+    return fused(*args) if fits(lax.axis_size("wide"), args) else general(*args)
 
 
 def solution(mesh):

time: 191 us -> 54.3 us (0.28)
  blocking collectives: 144 us -> 0 us
  Pallas kernels: 0 us -> 49.7 us
  matrix products: 25.8 us -> 0 us
  starting transfers between devices: 12.7 us -> 0 us
  other arithmetic: 2.87 us -> 0 us
    all_to_all x1 -> x0, blocking collectives: 74.8 us -> none  [shards(): lax.all_to_all(outgoing, 'wide', split_axis=0, concat_axis=0, tiled=True)]
    psum x1 -> x0, blocking collectives: 69 us -> none  [shards(): projected = lax.psum(partial_rank, 'wide').astype(jnp.bfloat16)]
    pallas_call x0 -> x1, Pallas kernels: none -> 49.7 us  [fused(): pl.pallas_call(kernel, out_shape=jax.ShapeDtypeStruct((tokens // n, 2 * w...]
    dot_general x4 -> x0, matrix products: 25.8 us -> none  [the longest x1 21.9 us: shards(): jnp.dot(hidden_pieces, down_weight[0], preferred_element_type=jnp.float32)]
    all_to_all x1 -> x0, starting transfers between devices: 7.35 us -> none  [shards(): lax.all_to_all(turned, 'wide', split_axis=2, concat_axis=1, tiled=True)]
    ppermute x2 -> x0, starting transfers between devices: 5.31 us -> none  [swapped(): lax.ppermute(value, axis, [(i, i ^ 1 << distance) for i in range(lax.axis...]
    reduce_sum x2 -> x0, other arithmetic: 2.87 us -> none  [the longest x1 2.78 us: shards(): jnp.sum(received.reshape(FF_GROUPS, column_groups, rows_own, block_width)...]
    reshape x0 -> x2, local copies, waits for them, and re-layouts: none -> 2.72 us  [the longest x1 1.39 us: fused(): adapter_ids.reshape(tokens, 1)]
  transfers between devices with their start and end apart: 3 -> 0, of which waited for: 1 -> 0; matrix products, arithmetic and copies ran while one was open for 2% -> 0% of each run, Pallas kernels for 0% -> 0%
where the time goes in v1:
time: 54.3 us; the launch traced here: 54.1 us
  Pallas kernels  49.7 us (92%)
  local copies, waits for them, and re-layouts  4.34 us (8%)
    pallas_call x1, Pallas kernels, fused(): pl.pallas_call(kernel, out_shape=jax.ShapeDtypeStruct((tokens // n, 2 * w...  49.7 us
    unnamed x1, local copies, waits for them, and re-layouts  1.62 us
    reshape x1, local copies, waits for them, and re-layouts, fused(): adapter_ids.reshape(tokens, 1)  1.39 us
    reshape x1, local copies, waits for them, and re-layouts, fused(): core_slot.reshape(adapters, 1)  1.33 us

profile of v1, /device:TPU:1, one launch (start us, length us, event | category | flops | bytes accessed | tf_op | source)
XLA Modules:
  0.0 54.1 jit_solution(12308046112994813649)
XLA Ops:
  0.0 1.3 %copy.9.slot_col = s32[32,1]{1,0:T(8,128)} copy(s32[32,1]{0,1:T(1,128)} %bitcast.6) | data formatting | bytes 256 | tf_op jit(solution)/shard_map/reshape | solution.py:401
  1.3 1.4 %copy.8.ids_col = s32[128,1]{1,0:T(8,128)} copy(s32[128,1]{0,1:T(1,128)} %bitcast.4) | data formatting | bytes 1024 | tf_op jit(solution)/shard_map/reshape | solution.py:400
  2.7 49.7 %shard_map.73 = bf16[8,12288]{1,0:T(8,128)(2,1)} custom-call(s32[128,1]{1,0:T(8,128)} %copy.8.ids_col, s32[1,128]{1,0:T(1,128)} %bitcast.5, s32[32,1]{1,0:T(8,128)} %copy.9.slot_col, s32[1,32]{1,0:T(1,128)} %bitcast.7, bf16[128,1792]{1,0:T(8,128)(2,1)} %hidden.1, bf16[1,3584,6144]{2,1,0:T(8,128)(2,1)} %weight.1, bf16[1792,512]{1,0:T(8,128)(2,1)} %rank_in.1, ...), custom_call_target="tpu_custom_call" | custom-call | flops 5637144576 | bytes 44040192 | tf_op jit(solution)/shard_map/pallas_call | solution.py:364
  52.5 1.6 %copy.11 = bf16[8,12288]{1,0:T(8,128)(2,1)} copy(bf16[8,12288]{1,0:T(8,128)(2,1)} %shard_map.73) | data formatting | bytes 393216

commit v2 on v1

--- a/solution.py
+++ b/solution.py
@@ -6,7 +6,7 @@
 from jax.sharding import PartitionSpec as P
 
 FF_GROUPS = 8
-WINDOW = 3
+WINDOW = 4
 
 
 def swapped(value, axis, distance):
@@ -76,6 +76,7 @@
 
 CHUNK = 768
 HELD = 6
+EARLY, SECOND = 2, 4
 OWNER_CAP = 32
 MESH = pl.DeviceIdType.MESH
 F32, BF16 = jnp.float32, jnp.bfloat16
@@ -88,11 +89,11 @@
 
 
 def kernel(
-    ids_col, ids_row, slot_col, slot_row, hidden, weight, rank_in, rank_out, cores, out,
+    ids_row, slot_row, hidden, weight, rank_in, rank_out, cores, out,
     hid, wbuf, rin, core_buf, vbuf, acc, pstage, precv, proj, projected, lstage, lrecv,
-    ystage, yrecv, zstage, zrecv, fin, frecv,
+    ystage, yown, yrecv, zstage, zrecv, fin, frecv,
     load_sem, w_sem, h_sem, ps_sem, pr_sem, as_sem, ar_sem, ls_sem, lr_sem,
-    ys_sem, yr_sem, zs_sem, zr_sem, fs_sem, fr_sem,
+    ys_sem, yr_sem, zs_sem, zr_sem, fs_sem, fr_sem, vs_sem, vr_sem,
 ):
     n = 2 * FF_GROUPS
     me = lax.axis_index("wide")
@@ -117,16 +118,16 @@
     hid_copy.start()
     rin_copy = pltpu.make_async_copy(rank_in, rin, load_sem.at[1])
     rin_copy.start()
-    for k in range(WINDOW):
-        w_copy(k).start()
-    core_copy = pltpu.make_async_copy(cores, core_buf, load_sem.at[2])
-    core_copy.start()
     half = lax.rem(group, 2)
     spare = pl.ds(pl.multiple_of((1 - half) * rank_rows, rank_rows), rank_rows)
-    vbuf[spare, :] = jnp.zeros((rank_rows, vbuf.shape[1]), BF16)
+    vbuf[spare, EARLY * CHUNK :] = jnp.zeros((rank_rows, vbuf.shape[1] - EARLY * CHUNK), BF16)
     own_rank = pl.ds(pl.multiple_of(half * rank_rows, rank_rows), rank_rows)
     v_copy = pltpu.make_async_copy(rank_out.at[0], vbuf.at[own_rank, :], load_sem.at[3])
     v_copy.start()
+    for k in range(WINDOW):
+        w_copy(k).start(priority=1)
+    core_copy = pltpu.make_async_copy(cores, core_buf, load_sem.at[2])
+    core_copy.start()
 
     barrier = pltpu.get_barrier_semaphore()
 
@@ -134,58 +135,31 @@
     def _(d):
         pl.semaphore_signal(barrier, inc=1, device_id={"wide": lax.rem(me + d, n)}, device_id_type=MESH)
 
-    pl.semaphore_wait(barrier, n - 1)
 
     hid_copy.wait()
-    h_send = remote(hid.at[:, own_units], hid.at[:, own_units], h_sem.at[0], h_sem.at[1], sibling)
-    h_send.start()
-
     rin_copy.wait()
     partial_rank = jnp.dot(hid[:, own_units], rin[...], preferred_element_type=F32).astype(BF16)
     for c in range(FF_GROUPS):
         for s in range(2):
             pstage[2 * c + s] = partial_rank[16 * c : 16 * c + 16, 256 * s : 256 * s + 256]
 
-    def p_copy(d):
-        target = lax.rem(me + d, n)
-        return remote(pstage.at[target], precv.at[me], ps_sem.at[target], pr_sem.at[me], target)
-
-    def p_arrival(d):
-        source = lax.rem(me + d, n)
-        return remote(pstage.at[me], precv.at[source], ps_sem.at[source], pr_sem.at[source], source)
-
-    @pl.loop(1, n)
-    def _(d):
-        p_copy(d).start()
-
-    precv[me] = pstage[me]
-
-    def start_next(k):
-        @pl.when(k + WINDOW < chunks)
-        def _():
-            w_copy(k + WINDOW).start()
-
-    def product(k):
-        w_copy(k).wait()
-        start_next(k)
-        return jnp.dot(hid[...], wbuf[k], preferred_element_type=F32)
-
-    def hold(first, last):
-        @pl.loop(first, last)
-        def _(k):
-            acc[k] = product(k)
-
     def number(mask):
         return jnp.where(mask, 1.0, 0.0)
 
-    all_a = slot_col.shape[0]
+    def column(row):
+        size = row.shape[1]
+        eye = lax.broadcasted_iota(jnp.int32, (size, size), 0) == lax.broadcasted_iota(jnp.int32, (size, size), 1)
+        return jnp.sum(jnp.where(eye, row.astype(F32), 0.0), axis=1, keepdims=True).astype(jnp.int32)
+
+    all_a = slot_row.shape[1]
+    ids_col, slot_col = column(ids_row[...]), column(slot_row[...])
     lanes_a = lax.broadcasted_iota(jnp.int32, (tokens, all_a), 1)
     rows_a = lax.broadcasted_iota(jnp.int32, (all_a, tokens), 0)
     slots_c = jnp.sum(
-        jnp.where(ids_col[...] == lanes_a, slot_row[...].astype(F32), 0.0), axis=1, keepdims=True
+        jnp.where(ids_col == lanes_a, slot_row[...].astype(F32), 0.0), axis=1, keepdims=True
     ).astype(jnp.int32)
     slots_r = jnp.sum(
-        jnp.where(ids_row[...] == rows_a, slot_col[...].astype(F32), 0.0), axis=0, keepdims=True
+        jnp.where(ids_row[...] == rows_a, slot_col.astype(F32), 0.0), axis=0, keepdims=True
     ).astype(jnp.int32)
     owner_c = lax.div(slots_c, jnp.int32(adapters))
     owner_r = lax.div(slots_r, jnp.int32(adapters))
@@ -199,8 +173,62 @@
     picked_slot = jnp.sum(mine * slots_r.astype(F32), axis=1, keepdims=True).astype(jnp.int32)
     lanes_s = lax.broadcasted_iota(jnp.int32, (tokens, n * OWNER_CAP), 1)
 
+    pl.semaphore_wait(barrier, n - 1)
+    h_send = remote(hid.at[:, own_units], hid.at[:, own_units], h_sem.at[0], h_sem.at[1], sibling)
+    h_send.start()
+
+    def p_copy(d):
+        target = lax.rem(me + d, n)
+        return remote(pstage.at[target], precv.at[me], ps_sem.at[target], pr_sem.at[me], target)
+
+    def p_arrival(d):
+        source = lax.rem(me + d, n)
+        return remote(pstage.at[me], precv.at[source], ps_sem.at[source], pr_sem.at[source], source)
+
+    @pl.loop(1, n)
+    def _(d):
+        p_copy(d).start()
+
+    precv[me] = pstage[me]
+    v_copy.wait()
+
+    def v_move(k, rows):
+        part = vbuf.at[rows, pl.ds(pl.multiple_of(k * CHUNK, CHUNK), CHUNK)]
+        return remote(part, part, vs_sem.at[k], vr_sem.at[k], y_partner)
+
+    for k in range(EARLY):
+        v_move(k, own_rank).start()
+
+    def start_next(k):
+        @pl.when(k + WINDOW < chunks)
+        def _():
+            w_copy(k + WINDOW).start(priority=1)
+
+    def product(k):
+        w_copy(k).wait()
+        start_next(k)
+        return jnp.dot(hid[...], wbuf[k], preferred_element_type=F32)
+
+    def hold(first, last):
+        @pl.loop(first, last)
+        def _(k):
+            acc[k] = product(k)
+
     h_send.wait()
-    hold(0, 2)
+    def y_copy(k):
+        return remote(ystage.at[k], yrecv.at[k], ys_sem.at[k], yr_sem.at[k], y_partner)
+
+    def send_y(k, value):
+        for c in range(0, FF_GROUPS, 2):
+            even, odd = value[16 * c : 16 * c + 16], value[16 * c + 16 : 16 * c + 32]
+            ystage[k, c // 2] = jnp.where(yy == 0, odd, even).astype(BF16)
+            yown[k, c // 2] = jnp.where(yy == 0, even, odd)
+        y_copy(k).start()
+
+    @pl.loop(0, EARLY)
+    def _(k):
+        send_y(k, product(k))
+
 
     @pl.loop(1, n)
     def _(d):
@@ -223,7 +251,7 @@
     def _(d):
         a_copy(d).start()
 
-    hold(2, 4)
+    hold(EARLY, SECOND)
 
     @pl.loop(1, n)
     def _(d):
@@ -255,7 +283,7 @@
         l_copy(d).start()
 
     lrecv[me] = lstage[lax.div(me, 4)]
-    hold(4, HELD)
+    hold(SECOND, HELD)
 
     @pl.loop(1, n)
     def _(d):
@@ -263,18 +291,17 @@
 
     expand = number(owner_c * OWNER_CAP + place_c == lanes_s).astype(BF16)
     arrived = lrecv[...].reshape(n * OWNER_CAP, 128)
-    lowrank = jnp.dot(expand, arrived, preferred_element_type=F32).astype(BF16)
-    v_copy.wait()
-
-    def y_copy(k):
-        return remote(ystage.at[k, 1 - yy], yrecv.at[k], ys_sem.at[k], yr_sem.at[k], y_partner)
-
-    def send_y(k, value):
+    lowrank = jnp.dot(expand, arrived, preferred_element_type=F32)
+    kept = []
+    for c in range(0, FF_GROUPS, 2):
+        kept.append(jnp.where(yy == 0, lowrank[16 * c : 16 * c + 16], lowrank[16 * c + 16 : 16 * c + 32]))
+    kept = jnp.concatenate(kept, 0).astype(BF16)
+    lowrank = lowrank.astype(BF16)
+
+    def adapter_term(rows, k):
         cols = pl.ds(pl.multiple_of(k * CHUNK, CHUNK), CHUNK)
-        value = (value + jnp.dot(lowrank, vbuf[:, cols], preferred_element_type=F32)).astype(BF16)
-        for c in range(FF_GROUPS):
-            ystage[k, c % 2, c // 2] = value[16 * c : 16 * c + 16]
-        y_copy(k).start()
+        return jnp.dot(rows, vbuf[:, cols], preferred_element_type=F32)
+
 
     def z_copy(k, d):
         z_to = lax.rem(zz + d, 4)
@@ -288,12 +315,16 @@
             zstage.at[k, zz], zrecv.at[k, z_from], zs_sem.at[k, z_from], zr_sem.at[k, z_from], z_from * 4 + lax.rem(me, 4)
         )
 
-    def turn(k):
+    def turn(k, early):
         y_copy(k).wait_recv()
-        zstage[k] = (ystage[k, yy].astype(F32) + yrecv[k].astype(F32)).astype(BF16)
+        pair = yown[k] + yrecv[k].astype(F32)
+        if early:
+            v_move(k, spare).wait_recv()
+            pair += adapter_term(kept, k).reshape(pair.shape)
+        zstage[k] = pair.astype(BF16)
+        yown[k] = pair
         for d in range(1, 4):
             z_copy(k, d).start()
-        zrecv[k, zz] = zstage[k, zz]
 
     def f_copy(k):
         return remote(fin.at[k], frecv.at[k], fs_sem.at[k], fr_sem.at[k], sibling)
@@ -301,26 +332,30 @@
     def finish(k):
         for d in range(1, 4):
             z_arrival(k, d).wait_recv()
-        fin[k] = jnp.sum(zrecv[k].astype(F32), axis=0).astype(BF16)
+        value = yown[k, zz]
+        for d in range(1, 4):
+            value += zrecv[k, lax.rem(zz + d, 4)].astype(F32)
+        fin[k] = value.astype(BF16)
         f_copy(k).start()
 
-    @pl.loop(0, HELD)
-    def _(k):
-        send_y(k, acc[k])
+    @pl.loop(EARLY, HELD)
+    def _(k):
+        send_y(k, acc[k] + adapter_term(lowrank, k))
+
+    @pl.loop(0, EARLY)
+    def _(k):
+        turn(k, True)
 
     @pl.loop(HELD, chunks)
     def _(k):
-        send_y(k, product(k))
-        turn(k - HELD)
-
-    turned = chunks - HELD
-
-    @pl.loop(turned, chunks)
-    def _(k):
-        turn(k)
-        finish(k - turned)
-
-    @pl.loop(chunks - turned, chunks)
+        send_y(k, product(k) + adapter_term(lowrank, k))
+
+    @pl.loop(EARLY, chunks)
+    def _(k):
+        turn(k, False)
+        finish(k - EARLY)
+
+    @pl.loop(chunks - EARLY, chunks)
     def _(k):
         finish(k)
 
@@ -342,6 +377,9 @@
         p_copy(d).wait_send()
         a_copy(d).wait_send()
         l_copy(d).wait_send()
+
+    for k in range(EARLY):
+        v_move(k, own_rank).wait_send()
 
     @pl.loop(0, chunks)
     def _(k):
@@ -364,7 +402,7 @@
     return pl.pallas_call(
         kernel,
         out_shape=jax.ShapeDtypeStruct((tokens // n, 2 * width), BF16),
-        in_specs=[local] * 4 + [anywhere] * 5,
+        in_specs=[local] * 2 + [anywhere] * 5,
         out_specs=local,
         scratch_shapes=[
             pltpu.VMEM((tokens, rows), BF16),
@@ -379,7 +417,8 @@
             pltpu.VMEM((tokens, rank), BF16),
             pltpu.VMEM((rank // 128, OWNER_CAP, 128), BF16),
             pltpu.VMEM((n, OWNER_CAP, 128), BF16),
-            pltpu.VMEM((chunks, 2, 4, 16, CHUNK), BF16),
+            pltpu.VMEM((chunks, 4, 16, CHUNK), BF16),
+            pltpu.VMEM((chunks, 4, 16, CHUNK), F32),
             pltpu.VMEM((chunks, 4, 16, CHUNK), BF16),
             pltpu.VMEM((chunks, 4, 16, CHUNK), BF16),
             pltpu.VMEM((chunks, 4, 16, CHUNK), BF16),
@@ -388,7 +427,7 @@
             dma((4,)), dma((chunks,)), dma((2,)),
             dma((n,)), dma((n,)), dma((n,)), dma((n,)), dma((n,)), dma((n,)),
             dma((chunks,)), dma((chunks,)), dma((chunks, 4)), dma((chunks, 4)),
-            dma((chunks,)), dma((chunks,)),
+            dma((chunks,)), dma((chunks,)), dma((EARLY,)), dma((EARLY,)),
         ],
         compiler_params=pltpu.CompilerParams(
             collective_id=0, has_side_effects=True, vmem_limit_bytes=60 * 1024 * 1024
@@ -397,8 +436,7 @@
             flops=2 * tokens * rows * width, bytes_accessed=2 * rows * width, transcendentals=0
         ),
     )(
-        adapter_ids.reshape(tokens, 1), adapter_ids.reshape(1, tokens),
-        core_slot.reshape(adapters, 1), core_slot.reshape(1, adapters),
+        adapter_ids.reshape(1, tokens), core_slot.reshape(1, adapters),
         hidden, down_weight, rank_in, rank_out, cores,
     )
 

time: 54.3 us -> 50.2 us (0.924)
  local copies, waits for them, and re-layouts: 4.34 us -> 1.62 us
  Pallas kernels: 49.7 us -> 48.5 us
    reshape x2 -> x0, local copies, waits for them, and re-layouts: 2.72 us -> none  [the longest x1 1.39 us: fused(): adapter_ids.reshape(tokens, 1)]
    pallas_call x1, Pallas kernels: 49.7 us -> 48.5 us  [fused(): pl.pallas_call(kernel, out_shape=jax.ShapeDtypeStruct((tokens // n, 2 * w...]
where the time goes in v2:
time: 50.2 us; the launch traced here: 50.1 us
  Pallas kernels  48.5 us (97%)
  local copies, waits for them, and re-layouts  1.62 us (3%)
    pallas_call x1, Pallas kernels, fused(): pl.pallas_call(kernel, out_shape=jax.ShapeDtypeStruct((tokens // n, 2 * w...  48.5 us
    unnamed x1, local copies, waits for them, and re-layouts  1.62 us

profile of v2, /device:TPU:1, one launch (start us, length us, event | category | flops | bytes accessed | tf_op | source)
XLA Modules:
  0.0 50.1 jit_solution(15759988928639517980)
XLA Ops:
  0.0 48.5 %shard_map.73 = bf16[8,12288]{1,0:T(8,128)(2,1)} custom-call(s32[1,128]{1,0:T(1,128)} %bitcast.2, s32[1,32]{1,0:T(1,128)} %bitcast.3, bf16[128,1792]{1,0:T(8,128)(2,1)} %hidden.1, bf16[1,3584,6144]{2,1,0:T(8,128)(2,1)} %weight.1, bf16[1792,512]{1,0:T(8,128)(2,1)} %rank_in.1, bf16[1,64,6144]{2,1,0:T(8,128)(2,1)} %rank_out.1, bf16[2,512,512]{2,1,0:T(8,128)(2,1)} %cores.1), custom_call_target="tpu_custom_call" | custom-call | flops 5637144576 | bytes 44040192 | tf_op jit(solution)/shard_map/pallas_call | solution.py:402
  48.5 1.6 %copy.9 = bf16[8,12288]{1,0:T(8,128)(2,1)} copy(bf16[8,12288]{1,0:T(8,128)(2,1)} %shard_map.73) | data formatting | bytes 393216

commit v3 on v2

--- a/solution.py
+++ b/solution.py
@@ -6,7 +6,7 @@
 from jax.sharding import PartitionSpec as P
 
 FF_GROUPS = 8
-WINDOW = 4
+WINDOW = 3
 
 
 def swapped(value, axis, distance):
@@ -74,9 +74,9 @@
     return layer_out.astype(jnp.bfloat16)
 
 
-CHUNK = 768
-HELD = 6
-EARLY, SECOND = 2, 4
+CHUNK = 1024
+HELD = 5
+EARLY, SECOND = 1, 3
 OWNER_CAP = 32
 MESH = pl.DeviceIdType.MESH
 F32, BF16 = jnp.float32, jnp.bfloat16

time: 50.2 us -> 48.4 us (0.964)
  Pallas kernels: 48.5 us -> 46.6 us
    pallas_call x1, Pallas kernels: 48.5 us -> 46.6 us  [fused(): pl.pallas_call(kernel, out_shape=jax.ShapeDtypeStruct((tokens // n, 2 * w...]
where the time goes in v3:
time: 48.4 us; the launch traced here: 48.2 us
  Pallas kernels  46.6 us (96%)
  local copies, waits for them, and re-layouts  1.62 us (3%)
    pallas_call x1, Pallas kernels, fused(): pl.pallas_call(kernel, out_shape=jax.ShapeDtypeStruct((tokens // n, 2 * w...  46.6 us
    unnamed x1, local copies, waits for them, and re-layouts  1.62 us

profile of v3, /device:TPU:1, one launch (start us, length us, event | category | flops | bytes accessed | tf_op | source)
XLA Modules:
  0.0 48.2 jit_solution(47396863770519156)
XLA Ops:
  0.0 46.6 %shard_map.73 = bf16[8,12288]{1,0:T(8,128)(2,1)} custom-call(s32[1,128]{1,0:T(1,128)} %bitcast.2, s32[1,32]{1,0:T(1,128)} %bitcast.3, bf16[128,1792]{1,0:T(8,128)(2,1)} %hidden.1, bf16[1,3584,6144]{2,1,0:T(8,128)(2,1)} %weight.1, bf16[1792,512]{1,0:T(8,128)(2,1)} %rank_in.1, bf16[1,64,6144]{2,1,0:T(8,128)(2,1)} %rank_out.1, bf16[2,512,512]{2,1,0:T(8,128)(2,1)} %cores.1), custom_call_target="tpu_custom_call" | custom-call | flops 5637144576 | bytes 44040192 | tf_op jit(solution)/shard_map/pallas_call | solution.py:402
  46.6 1.6 %copy.9 = bf16[8,12288]{1,0:T(8,128)(2,1)} copy(bf16[8,12288]{1,0:T(8,128)(2,1)} %shard_map.73) | data formatting | bytes 393216
